TPU v7x, 32 devices: a whole 2x2x4 slice. The times are simulated.
32 devices in a mesh: depth: 4 (over y, x), tile: 8 (over z, core).
Axes of the slice: x: 2, y: 2, z: 4, core: 2. Of those that a mesh axis runs over, the one named last changes fastest.
Arguments:
- source: bfloat16 [16, 2, 128, 256], P('tile'), may hold values from -6 to 6
- anchors: int32 [16], P('tile'), may hold values from -256 to 1792, as said below
- counts: int32 [4], P('depth'), may hold values from 1 to 3, 8 in all
- reflect: bfloat16 [4, 3, 128, 2048], P('depth', None, None, 'tile'), may hold values from -0.3984375 to 0.3984375
- lateral_x: bfloat16 [4, 3, 2, 128, 128], P('depth'), may hold values from -0.375 to 0.375
- lateral_y: bfloat16 [4, 3, 2, 256, 256], P('depth'), may hold values from -0.25 to 0.25
Outputs:
- image: float32 [4, 3, 128, 2048], P('depth', None, None, 'tile')
Inputs may be any that keep to these rules, and one draw needn't show every extreme that they name: `anchors`: the shots held by tile index t start their aperture between (t - 1) * 256 and t * 256. The counts sum to 8; slots at or past a section's count are unused.
All inputs are finite; a program needn't handle non-finite values. No bound on the sum of `counts` on one device may be relied on, other than what follows from the above.
Results may differ from a plain program's by a relative error of at most 0.023.
Values may be sent and summed in bfloat16 or wider, within the bound.
No kernel may reach another device: no remote copies, remote signals or barrier semaphores. Data moves between devices by JAX's collectives and lax.ppermute only.
A program may use at most 64 MiB of HBM per device.

v0:
```python
import functools

import jax
import jax.numpy as jnp
from jax import lax
from jax.experimental import pallas as pl
from jax.experimental.pallas import tpu as pltpu
from jax.sharding import PartitionSpec as P

BOTH = ("depth", "tile")
MIB = 1024 * 1024
TAIL = 16


class Plan:
    def __init__(self, shots):
        self.sections = lax.axis_size("depth")
        self.tiles = lax.axis_size("tile")
        self.shots = shots
        self.group = self.sections // shots
        assert self.sections == 4 and self.group * shots == self.sections
        assert self.tiles % (2 * self.group) == 0

    def device(self, depth, tile):
        return depth * self.tiles + tile

    def bases(self):
        return range(0, self.tiles, self.group)

    def worker(self, base, w):
        return self.device(w, base + w // self.shots)

    def other(self, w, base):
        return self.device(w, base + (w // self.shots + 1) % self.group)

    def ops_to_workers(self, r):
        return [
            (self.other(w ^ r, base), self.worker(base, w))
            for base in self.bases()
            for w in range(self.sections)
        ]

    def swap_workers(self):
        return [
            (self.worker(base, w), self.worker((base // self.group ^ 1) * self.group, w))
            for base in self.bases()
            for w in range(self.sections)
        ]

    def to_workers(self, r):
        return [
            (self.device(w ^ r, base + w // self.shots), self.worker(base, w))
            for base in self.bases()
            for w in range(self.sections)
        ]

    def from_workers(self, r):
        return [(b, a) for a, b in self.to_workers(r)]


def pack_kernel(group, sizes, x_hbm, y_hbm, even, odd, late, half_out, x_ref, y_ref, sem):
    slots, rows, columns = sizes
    loads = [
        pltpu.make_async_copy(x_hbm, x_ref, sem.at[0]),
        pltpu.make_async_copy(y_hbm, y_ref, sem.at[1]),
    ]
    for load in loads:
        load.start()
    for load in loads:
        load.wait()
    piece = rows // 2
    part = columns + piece
    first = (slots - 1) * part
    for half in range(2):
        for slot in range(slots):
            op_x = jnp.concatenate(
                [x_ref[slot, i, half * piece : (half + 1) * piece, :] for i in range(2)], axis=1
            )
            op_y = y_ref[slot, half]
            if slot < slots - 1:
                places = [(out, half * first + slot * part) for out in (even, odd)]
            else:
                places = [(late, half * part)]
            for out, spot in places:
                out[spot : spot + columns, :] = op_y
                out[spot + columns : spot + part, :] = op_x
    plane = lax.rem(lax.axis_index("tile") // group, 2)
    half_out[:first, :] = even[pl.ds(pl.multiple_of(plane * first, first), first), :]
    half_out[first:, :] = late[pl.ds(pl.multiple_of(plane * part, part), part), :]


def window_kernel(shots, sizes, anchors_hbm, counts, left_ref, right_hbm, *refs):
    slots, rows, columns = sizes
    messages, (alone, anchors, right_ref, sem) = refs[shots : 2 * shots], refs[2 * shots :]
    loads = [
        pltpu.make_async_copy(anchors_hbm, anchors, sem.at[0]),
        pltpu.make_async_copy(right_hbm, right_ref, sem.at[1]),
    ]
    for load in loads:
        load.start()
    for load in loads:
        load.wait()
    section, tile = lax.axis_index("depth"), lax.axis_index("tile")
    left, right = left_ref[...].astype(jnp.float32), right_ref[...].astype(jnp.float32)
    lanes = lax.broadcasted_iota(jnp.int32, left.shape, 1)
    tail = jnp.full((TAIL, columns), counts[0].astype(jnp.float32), jnp.float32)
    for q, message in enumerate(messages):
        offset = anchors[lax.rem(section, shots) ^ q] - (tile - 1) * columns
        merged = jnp.where(lanes >= offset, left, right)
        back = lax.rem(columns - lax.rem(offset, columns), columns)
        window = pltpu.roll(merged, back, 1).astype(message.dtype)
        for out in [message] + ([alone] if q == shots - 1 else []):
            spot = out.shape[0] - TAIL - slots * rows
            out[spot : spot + slots * rows, :] = window
            out[spot + slots * rows :, :] = tail.astype(out.dtype)


class Sweep:
    def __init__(self, shots, group, sizes, turned_y, turned_x, level_w, waves, stage_y, stage_x):
        self.sizes = sizes
        self.turned_y, self.turned_x, self.level_w = turned_y, turned_x, level_w
        self.waves, self.stage_y, self.stage_x = waves, stage_y, stage_x
        slots, rows, columns = sizes
        self.piece = rows // 2
        self.part = columns + self.piece
        self.first = (slots - 1) * self.part
        self.half_rows = self.first + self.part
        self.win_rows = slots * rows + TAIL
        self.here, tile = lax.axis_index("depth"), lax.axis_index("tile")
        self.shot = lax.rem(self.here, shots)
        self.is_worker = (self.here // shots == lax.rem(tile, group)).astype(jnp.int32)

    def window_start(self, window_ref):
        return window_ref.shape[0] - self.win_rows

    def fetch(self, r, slot, place, sources):
        slots, rows, columns = self.sizes
        for r_of, (early, late, window) in enumerate(sources):
            early_slots = slots if early.shape[0] == 2 * self.half_rows else slots - 1
            choices = [(early, early_slots * self.part, slot < early_slots, slot)]
            if late is not None:
                choices.append((late, self.part, slot == slots - 1, 0))
            for ref, stride, chosen, at in choices:

                @pl.when((r == r_of) & chosen)
                def _():
                    for half in range(2):
                        start = pl.multiple_of(half * stride + at * self.part, self.piece)
                        self.stage_y[half * columns : (half + 1) * columns, :] = ref[
                            pl.ds(start, columns), :
                        ]
                        tail = pl.multiple_of(start + columns, self.piece)
                        self.stage_x[half * self.piece : (half + 1) * self.piece, :] = ref[
                            pl.ds(tail, self.piece), :
                        ]
                    spot = self.window_start(window) + slot * rows
                    self.level_w[place] = window[pl.ds(pl.multiple_of(spot, TAIL), rows), :]

    def blocks(self, re, im):
        upper = jnp.concatenate([re, -im], axis=1)
        return jnp.concatenate([upper, jnp.concatenate([im, re], axis=1)], axis=0)

    def complex_sum(self, both):
        _, rows, columns = self.sizes
        with_re, with_im = both[:, :columns], both[:, columns:]
        return with_re[:rows] - with_im[rows:], with_im[:rows] + with_re[rows:]

    def dot(self, a, b, dims):
        return lax.dot_general(a, b, (dims, ((), ())), preferred_element_type=jnp.float32)

    def down(self, place):
        _, rows, columns = self.sizes
        x_re, x_im = self.stage_x[:, :rows], self.stage_x[:, rows:]
        wave = self.waves[place].astype(jnp.float32)
        gain = 1.0 + self.level_w[place].astype(jnp.float32)
        scaled = jnp.concatenate([gain * wave[:rows], gain * wave[rows:]], axis=0)
        self.turned_x[place] = self.blocks(x_re.T, x_im.T)
        middle = self.dot(self.blocks(x_re, x_im), scaled.astype(jnp.bfloat16), ((1,), (0,)))
        for i in range(2):
            lines = slice(i * columns, (i + 1) * columns)
            self.turned_y[place, lines, :] = self.stage_y[lines, :].T
        both = self.dot(middle.astype(jnp.bfloat16), self.stage_y[...], ((1,), (1,)))
        moved = jnp.concatenate(self.complex_sum(both), axis=0)
        self.waves[place + 1] = moved.astype(jnp.bfloat16)
        return place + 1

    def up(self, r, slot, place, wave_up, outs):
        _, rows, columns = self.sizes
        level = place - 1
        wave = self.waves[level].astype(jnp.float32)
        window = self.level_w[level].astype(jnp.float32)
        back = self.dot(self.turned_x[level], wave_up[...], ((1,), (0,)))
        both = self.dot(back.astype(jnp.bfloat16), self.turned_y[level], ((1,), (1,)))
        spread_re, spread_im = self.complex_sum(both)
        up_re = (window * wave[:rows] + spread_re).astype(jnp.bfloat16)
        up_im = (window * wave[rows:] + spread_im).astype(jnp.bfloat16)
        wave_up[:rows] = up_re
        wave_up[rows:] = up_im
        product = wave[:rows] * up_re.astype(jnp.float32)
        product += wave[rows:] * up_im.astype(jnp.float32)
        spot = pl.multiple_of(slot * rows, rows)
        for r_of, out in enumerate(outs):

            @pl.when(r == r_of)
            def _():
                out[pl.ds(spot, rows), :] = product.astype(out.dtype)

        return level


def down_kernel(sections, shots, group, sizes, source_ref, *refs):
    slots, rows, _ = sizes
    (own, near, far), (own_late, joined, far_window) = refs[:3], refs[3:6]
    *buffers, state, stage_y, stage_x = refs[6:]
    it = Sweep(shots, group, sizes, *buffers, stage_y, stage_x)
    waves = it.waves
    sources = [
        (own, own_late, own),
        (near, None, near),
        (far, None, far),
        (joined, None, far_window),
    ]

    @pl.when(it.is_worker == 0)
    def _():
        for i in range(3 + sections):
            state[i] = 0

    @pl.when(it.is_worker != 0)
    def _():
        waves[0] = source_ref[it.shot]
        for r, (_, _, window) in enumerate(sources):
            value = jnp.max(window[window.shape[0] - TAIL :, :].astype(jnp.float32))
            state[3 + r] = value.astype(jnp.int32)

        def section_down(section, carry):
            place, going, next_section, next_slot = carry
            r = section ^ it.here
            partial = (r != 0) & (r != sections - 1)
            count = state[3 + r]
            ready = jnp.where(partial, jnp.minimum(count, slots - 1), count)

            def level_down(slot, place):
                it.fetch(r, slot, place, sources)
                return it.down(place)

            place = lax.fori_loop(0, jnp.where(going, ready, 0), level_down, place)
            whole = ready == count
            next_section = jnp.where(going, jnp.where(whole, section + 1, section), next_section)
            next_slot = jnp.where(going, jnp.where(whole, 0, ready), next_slot)
            return place, going & whole, next_section, next_slot

        zero = jnp.int32(0)
        carry = (zero, jnp.bool_(True), zero, zero)
        place, _, next_section, next_slot = lax.fori_loop(0, sections, section_down, carry)
        state[0] = next_section
        state[1] = next_slot
        state[2] = place


def up_kernel(sections, shots, group, sizes, state, *refs):
    slots, rows, _ = sizes
    (own, near, far), (own_late, near_late, far_late, joined, far_window) = refs[:3], refs[3:8]
    outs, refs = refs[12 : 12 + sections], refs[12 + sections :]
    *buffers, stage_y, stage_x, wave_up = refs
    it = Sweep(shots, group, sizes, *buffers, stage_y, stage_x)
    sources = [
        (own, own_late, own),
        (near, near_late, near),
        (far, far_late, far),
        (joined, None, far_window),
    ]

    @pl.when(it.is_worker == 0)
    def _():
        outs[0][...] = jnp.zeros(outs[0].shape, outs[0].dtype)

    @pl.when(it.is_worker != 0)
    def _():
        for out in outs:
            out[...] = jnp.zeros(out.shape, out.dtype)
        wave_up[...] = jnp.zeros(wave_up.shape, wave_up.dtype)
        next_section, next_slot = state[0], state[1]

        def section_down(section, place):
            r = section ^ it.here
            begin = jnp.where(section == next_section, next_slot, 0)

            def level_down(slot, place):
                it.fetch(r, slot, place, sources)
                return it.down(place)

            return lax.fori_loop(begin, state[3 + r], level_down, place)

        last = lax.fori_loop(next_section, sections, section_down, state[2])

        def section_up(step, place):
            r = (sections - 1 - step) ^ it.here
            count = state[3 + r]
            return lax.fori_loop(
                0,
                count,
                lambda inner, place: it.up(r, count - 1 - inner, place, wave_up, outs),
                place,
            )

        lax.fori_loop(0, sections, section_up, last)


def join_kernel(group, first_ref, second_ref, out_ref):
    plane = lax.rem(lax.axis_index("tile") // group, 2)
    half_rows = first_ref.shape[0]
    for i, ref in enumerate((first_ref, second_ref)):
        start = pl.multiple_of((plane if i == 0 else 1 - plane) * half_rows, half_rows)
        out_ref[pl.ds(start, half_rows), :] = ref[...]


def hold_kernel(array_ref, after_ref, out_ref):
    pass


def place_kernel(shots, anchors, *refs):
    arrived, (left_out, own_out) = refs[:-2], refs[-2:]
    section, tile = lax.axis_index("depth"), lax.axis_index("tile")
    places, columns = left_out.shape
    left_sum, own_sum = None, None
    for q in range(shots):
        offset = anchors[lax.rem(section, shots) ^ q] - (tile - 1) * columns
        total = None
        for r in range(q, len(arrived), shots):
            value = arrived[r][:places, :].astype(jnp.float32)
            total = value if total is None else total + value
        turned = pltpu.roll(total, lax.rem(offset, columns), 1)
        lanes = lax.broadcasted_iota(jnp.int32, turned.shape, 1)
        left = jnp.where(lanes >= offset, turned, 0.0)
        own = jnp.where(lanes >= offset, 0.0, turned)
        left_sum = left if left_sum is None else left_sum + left
        own_sum = own if own_sum is None else own_sum + own
    left_out[...] = left_sum.astype(left_out.dtype)
    own_out[...] = own_sum


def kept(array):
    return pltpu.with_memory_space_constraint(array, pltpu.HBM)


def held(array):
    return pltpu.with_memory_space_constraint(array, pltpu.VMEM)


def on_device(source, anchors, counts, reflect, lateral_x, lateral_y):
    shots, _, rows, columns = source.shape
    slots = reflect.shape[1]
    sizes = (slots, rows, columns)
    plan = Plan(shots)
    sections, group = plan.sections, plan.group
    assert shots == 2
    bf16 = jnp.bfloat16
    smem = pl.BlockSpec(memory_space=pltpu.SMEM)
    vmem = pl.BlockSpec(memory_space=pltpu.VMEM)
    hbm = pl.BlockSpec(memory_space=pltpu.HBM)
    anywhere = pl.BlockSpec(memory_space=pl.ANY)

    def params(mib):
        return pltpu.CompilerParams(vmem_limit_bytes=mib * MIB)

    tile_reflect = reflect[0].reshape(slots * rows, columns)
    halo = lax.ppermute(tile_reflect, "tile", [(i, i + 1) for i in range(plan.tiles - 1)])
    part = columns + rows // 2
    half_rows, win_rows = slots * part, slots * rows + TAIL
    early_rows = 2 * (half_rows - part) + win_rows
    even = pltpu.VMEM((early_rows + 5 * TAIL, columns), bf16)
    odd = pltpu.VMEM((early_rows, columns), bf16)
    even_early, odd_early, late, far_half = pl.pallas_call(
        functools.partial(pack_kernel, group, sizes),
        out_shape=[
            even,
            odd,
            jax.ShapeDtypeStruct((2 * part, columns), bf16),
            jax.ShapeDtypeStruct((half_rows, columns), bf16),
        ],
        in_specs=[hbm, hbm],
        out_specs=[vmem] * 4,
        scratch_shapes=[
            pltpu.VMEM(lateral_x.shape[1:], bf16),
            pltpu.VMEM(lateral_y.shape[1:], bf16),
            pltpu.SemaphoreType.DMA((2,)),
        ],
        compiler_params=params(12),
        name="pack",
    )(kept(lateral_x[0]), kept(lateral_y[0]))
    last = sections - 1
    far_half = lax.ppermute(far_half, BOTH, plan.to_workers(last))
    even_early, odd_early, far_window = pl.pallas_call(
        functools.partial(window_kernel, shots, sizes),
        out_shape=[even, odd, jax.ShapeDtypeStruct((win_rows, columns), bf16)],
        in_specs=[hbm, smem, vmem, hbm, vmem, vmem],
        out_specs=[vmem] * 3,
        scratch_shapes=[
            pltpu.SMEM((shots,), jnp.int32),
            pltpu.VMEM((slots * rows, columns), bf16),
            pltpu.SemaphoreType.DMA((2,)),
        ],
        input_output_aliases={4: 0, 5: 1},
        compiler_params=params(12),
        cost_estimate=pl.CostEstimate(flops=3 * 10**9, bytes_accessed=4 * MIB, transcendentals=0),
        name="windows",
    )(kept(anchors), counts, halo, kept(tile_reflect), held(even_early), held(odd_early))
    messages = [
        even_early,
        lax.ppermute(odd_early, BOTH, plan.to_workers(1)),
        lax.ppermute(even_early, BOTH, plan.to_workers(2)),
    ]
    far_window = lax.ppermute(far_window, BOTH, plan.to_workers(last))
    other_half = lax.ppermute(far_half, BOTH, plan.swap_workers())
    late = pl.pallas_call(
        hold_kernel,
        out_shape=jax.ShapeDtypeStruct(late.shape, bf16),
        in_specs=[anywhere] * 2,
        out_specs=anywhere,
        input_output_aliases={0: 0},
        compiler_params=params(2),
        cost_estimate=pl.CostEstimate(flops=36 * 10**8, bytes_accessed=0, transcendentals=0),
        name="hold",
    )(late, far_window)
    lates = [lax.ppermute(late, BOTH, plan.ops_to_workers(r)) for r in (1, 2)]
    joined = pl.pallas_call(
        functools.partial(join_kernel, group),
        out_shape=pltpu.VMEM((2 * half_rows, columns), bf16),
        in_specs=[vmem] * 2,
        out_specs=vmem,
        compiler_params=params(8),
        name="join",
    )(held(far_half), held(other_half))

    levels = sections * slots
    buffers = [
        pltpu.VMEM((levels, 2 * columns, columns), bf16),
        pltpu.VMEM((levels, 2 * rows, 2 * rows), bf16),
        pltpu.VMEM((levels, rows, columns), bf16),
        pltpu.VMEM((levels + 1, 2 * rows, columns), bf16),
    ]
    stages = [pltpu.VMEM((2 * columns, columns), bf16), pltpu.VMEM((rows, 2 * rows), bf16)]
    messages = [held(message) for message in messages]
    late, joined, far_window = held(late), held(joined), held(far_window)
    *filled, state = pl.pallas_call(
        functools.partial(down_kernel, sections, shots, group, sizes),
        out_shape=buffers + [jax.ShapeDtypeStruct((3 + sections,), jnp.int32)],
        in_specs=[vmem] * 7,
        out_specs=[vmem] * 4 + [smem],
        scratch_shapes=stages,
        compiler_params=params(24),
        name="down",
    )(held(source.reshape(shots, 2 * rows, columns)), *messages, late, joined, far_window)
    correlations = pl.pallas_call(
        functools.partial(up_kernel, sections, shots, group, sizes),
        out_shape=[
            jax.ShapeDtypeStruct((slots * rows + TAIL * more, columns), bf16)
            for more in (0, 1, 0, 2)
        ]
        + buffers,
        in_specs=[smem] + [vmem] * 12,
        out_specs=[vmem] * (sections + 4),
        scratch_shapes=stages + [pltpu.VMEM((2 * rows, columns), bf16)],
        input_output_aliases={9 + i: sections + i for i in range(4)},
        compiler_params=params(24),
        name="up",
    )(
        state, *messages, late, *[held(part) for part in lates], joined, far_window,
        *[held(buffer) for buffer in filled],
    )

    corr_shape = jax.ShapeDtypeStruct((slots * rows, columns), bf16)
    arrived = [correlations[0]] + [
        lax.ppermute(correlations[r], BOTH, plan.from_workers(r)) for r in range(1, sections)
    ]
    left, own = pl.pallas_call(
        functools.partial(place_kernel, shots),
        out_shape=[corr_shape, jax.ShapeDtypeStruct((slots * rows, columns), jnp.float32)],
        in_specs=[smem] + [vmem] * sections,
        out_specs=[vmem, vmem],
        compiler_params=params(8),
        name="place",
    )(anchors, *arrived)
    from_right = lax.ppermute(left, "tile", [(i + 1, i) for i in range(plan.tiles - 1)])
    image = own + from_right.astype(jnp.float32)
    return image.reshape(1, slots, rows, columns)


def solution(mesh):
    return jax.shard_map(
        on_device,
        mesh=mesh,
        in_specs=(
            P("tile", None, None, None),
            P("tile"),
            P("depth"),
            P("depth", None, None, "tile"),
            P("depth", None, None, None, None),
            P("depth", None, None, None, None),
        ),
        out_specs=P("depth", None, None, "tile"),
        check_vma=False,
    )
```

profile of v0, /device:TPU:1, one launch (start us, length us, event | category | flops | bytes accessed | tf_op | source)
XLA Modules:
  0.0 56.5 jit_solution(15240240801421408854)
XLA Ops:
  0.0 4.6 %collective-permute-start = (bf16[384,256]{1,0:T(8,128)(2,1)}, bf16[384,256]{1,0:T(8,128)(2,1)S(1)}, u32[]{:S(2)}, u32[]{:S(2)}) collective-permute-start(bf16[384,256]{1,0:T(8,128)(2,1)} %bitcast.8), channel_id=1, source_target_pairs={{0,1},{1,2},{2,3},{3,4},{4,5},{5,6},{6,7},{8,9},{9,10},{10,11},{11... | collective-permute-start | bytes 589832 | tf_op jit(solution)/shard_map/ppermute | solution.py:368
  4.6 1.4 %pack.1 = (bf16[1760,256]{1,0:T(8,128)(2,1)S(1)}, bf16[1680,256]{1,0:T(8,128)(2,1)S(1)}, bf16[640,256]{1,0:T(8,128)(2,1)S(1)}, bf16[960,256]{1,0:T(8,128)(2,1)S(1)}) custom-call(bf16[3,2,128,128]{3,2,1,0:T(8,128)(2,1)} %bitcast.7, bf16[3,2,256,256]{3,2,1,0:T(8,128)(2,1)} %bitcast.6), custom_call_target="tpu_custom_call" | custom-call | tf_op jit(solution)/shard_map/pack/pallas_call | solution.py:374
  6.0 4.1 %collective-permute-start.4 = (bf16[960,256]{1,0:T(8,128)(2,1)S(1)}, bf16[960,256]{1,0:T(8,128)(2,1)S(1)}, u32[]{:S(2)}, u32[]{:S(2)}) collective-permute-start(bf16[960,256]{1,0:T(8,128)(2,1)S(1)} %get-tuple-element.29), channel_id=1, source_target_pairs={{24,0},{16,8},{9,17},{1,25},{26,2},{18,10},{11,19},{3,27},{28,4},{... | collective-permute-start | bytes 1474568 | tf_op jit(solution)/shard_map/ppermute | solution.py:393
  10.8 0.0 collective-permute-done.left_ref
  10.8 1.2 %windows.1 = (bf16[1760,256]{1,0:T(8,128)(2,1)S(1)}, bf16[1680,256]{1,0:T(8,128)(2,1)S(1)}, bf16[400,256]{1,0:T(8,128)(2,1)S(1)}) custom-call(s32[2]{0:T(128)} %anchors.1, s32[1]{0:T(128)S(6)} %copy.21.counts, bf16[384,256]{1,0:T(8,128)(2,1)S(1)} %collective-permute-done.left_ref, ...), custom_call_target="tpu_custom_call", output_to_operand_aliasing={{0}: (4, {}), {1}: (5, {})} | custom-call | flops 3000000000 | bytes 4194304 | tf_op jit(solution)/shard_map/windows/pallas_call | solution.py:394
  12.0 1.3 %collective-permute-start.2 = (bf16[1760,256]{1,0:T(8,128)(2,1)S(1)}, bf16[1760,256]{1,0:T(8,128)(2,1)S(1)}, u32[]{:S(2)}, u32[]{:S(2)}) collective-permute-start(bf16[1760,256]{1,0:T(8,128)(2,1)S(1)} %get-tuple-element.25.refs_0_), channel_id=1, source_target_pairs={{16,0},{24,8},{1,17},{9,25},{18,2},{26,10},{3,19},{11,27},{20,4},{... | collective-permute-start | bytes 2703368 | tf_op jit(solution)/shard_map/ppermute | solution.py:412
  13.3 1.3 %collective-permute-start.3 = (bf16[400,256]{1,0:T(8,128)(2,1)S(1)}, bf16[400,256]{1,0:T(8,128)(2,1)S(1)}, u32[]{:S(2)}, u32[]{:S(2)}) collective-permute-start(bf16[400,256]{1,0:T(8,128)(2,1)S(1)} %get-tuple-element.28), channel_id=1, source_target_pairs={{24,0},{16,8},{9,17},{1,25},{26,2},{18,10},{11,19},{3,27},{28,4},{... | collective-permute-start | bytes 614408 | tf_op jit(solution)/shard_map/ppermute | solution.py:414
  14.6 0.7 %collective-permute-start.1 = (bf16[1680,256]{1,0:T(8,128)(2,1)S(1)}, bf16[1680,256]{1,0:T(8,128)(2,1)S(1)}, u32[]{:S(2)}, u32[]{:S(2)}) collective-permute-start(bf16[1680,256]{1,0:T(8,128)(2,1)S(1)} %get-tuple-element.26), channel_id=1, source_target_pairs={{8,0},{0,8},{25,17},{17,25},{10,2},{2,10},{27,19},{19,27},{12,4},{... | collective-permute-start | bytes 2580488 | tf_op jit(solution)/shard_map/ppermute | solution.py:411
  15.4 1.8 %collective-permute-done.4.first_ref = bf16[960,256]{1,0:T(8,128)(2,1)S(1)} collective-permute-done((bf16[960,256]{1,0:T(8,128)(2,1)S(1)}, bf16[960,256]{1,0:T(8,128)(2,1)S(1)}, u32[]{:S(2)}, u32[]{:S(2)}) %collective-permute-start.4) | collective-permute-done | bytes 491552 | tf_op jit(solution)/shard_map/ppermute | solution.py:393
  17.1 0.7 %collective-permute-start.5 = (bf16[960,256]{1,0:T(8,128)(2,1)S(1)}, bf16[960,256]{1,0:T(8,128)(2,1)S(1)}, u32[]{:S(2)}, u32[]{:S(2)}) collective-permute-start(bf16[960,256]{1,0:T(8,128)(2,1)S(1)} %collective-permute-done.4.first_ref), channel_id=1, source_target_pairs={{0,2},{8,10},{17,19},{25,27},{2,0},{10,8},{19,17},{27,25},{4,6},{1... | collective-permute-start | bytes 1474568 | tf_op jit(solution)/shard_map/ppermute | solution.py:415
  17.8 3.7 %collective-permute-done.3.after_ref.refs_5_.refs_7_ = bf16[400,256]{1,0:T(8,128)(2,1)S(1)} collective-permute-done((bf16[400,256]{1,0:T(8,128)(2,1)S(1)}, bf16[400,256]{1,0:T(8,128)(2,1)S(1)}, u32[]{:S(2)}, u32[]{:S(2)}) %collective-permute-start.3) | collective-permute-done | bytes 204832 | tf_op jit(solution)/shard_map/ppermute | solution.py:414
  21.5 4.4 %collective-permute-start.7 = (bf16[640,256]{1,0:T(8,128)(2,1)S(1)}, bf16[640,256]{1,0:T(8,128)(2,1)S(1)}, u32[]{:S(2)}, u32[]{:S(2)}) collective-permute-start(bf16[640,256]{1,0:T(8,128)(2,1)S(1)} %hold.1.refs_3_), channel_id=1, source_target_pairs={{16,0},{24,8},{1,17},{9,25},{18,2},{26,10},{3,19},{11,27},{20,4},{... | collective-permute-start | bytes 983048 | tf_op jit(solution)/shard_map/ppermute | solution.py:426
  25.9 1.3 %collective-permute-start.6 = (bf16[640,256]{1,0:T(8,128)(2,1)S(1)}, bf16[640,256]{1,0:T(8,128)(2,1)S(1)}, u32[]{:S(2)}, u32[]{:S(2)}) collective-permute-start(bf16[640,256]{1,0:T(8,128)(2,1)S(1)} %hold.1.refs_3_), channel_id=1, source_target_pairs={{9,0},{1,8},{24,17},{16,25},{11,2},{3,10},{26,19},{18,27},{13,4},{... | collective-permute-start | bytes 983048 | tf_op jit(solution)/shard_map/ppermute | solution.py:426
  27.3 0.0 collective-permute-done.5.second_ref
  27.3 0.1 join.1.refs_4_.refs_6_
  27.4 0.0 collective-permute-done.1.refs_1_
  27.4 0.3 collective-permute-done.2.refs_2_
  27.7 0.0 copy-done
  27.7 0.6 %down.1 = (bf16[12,512,256]{2,1,0:T(8,128)(2,1)S(1)}, bf16[12,256,256]{2,1,0:T(8,128)(2,1)S(1)}, bf16[12,128,256]{2,1,0:T(8,128)(2,1)S(1)}, bf16[13,256,256]{2,1,0:T(8,128)(2,1)S(1)}, s32[7]{0:T(128)S(1)}) custom-call(bf16[2,256,256]{2,1,0:T(8,128)(2,1)S(1)} %bitcast.5, bf16[1760,256]{1,0:T(8,128)(2,1)S(1)} %get-tuple-element.25.refs_0_, ...), custom_call_target="tpu_custom_call" | custom-call | tf_op jit(solution)/shard_map/down/pallas_call | solution.py:446
  28.3 2.9 %collective-permute-done.7.refs_5_ = bf16[640,256]{1,0:T(8,128)(2,1)S(1)} collective-permute-done((bf16[640,256]{1,0:T(8,128)(2,1)S(1)}, bf16[640,256]{1,0:T(8,128)(2,1)S(1)}, u32[]{:S(2)}, u32[]{:S(2)}) %collective-permute-start.7) | collective-permute-done | bytes 327712 | tf_op jit(solution)/shard_map/ppermute | solution.py:426
  31.2 0.1 collective-permute-done.6.refs_4_
  31.2 0.6 %up.1 = (bf16[384,256]{1,0:T(8,128)(2,1)S(1)}, bf16[400,256]{1,0:T(8,128)(2,1)S(1)}, bf16[384,256]{1,0:T(8,128)(2,1)S(1)}, bf16[416,256]{1,0:T(8,128)(2,1)S(1)},...) custom-call(s32[7]{0:T(128)S(1)} %get-tuple-element.30.state, ...), custom_call_target="tpu_custom_call", output_to_operand_aliasing={{4}: (9, {}), {5}: (10, {}), {6}: (11, {}), {7}: (12, {})} | custom-call | tf_op jit(solution)/shard_map/up/pallas_call | solution.py:455
  31.8 1.3 %collective-permute-start.10 = (bf16[416,256]{1,0:T(8,128)(2,1)S(1)}, bf16[416,256]{1,0:T(8,128)(2,1)S(1)}, u32[]{:S(2)}, u32[]{:S(2)}) collective-permute-start(bf16[416,256]{1,0:T(8,128)(2,1)S(1)} %get-tuple-element.38), channel_id=1, source_target_pairs={{0,24},{8,16},{17,9},{25,1},{2,26},{10,18},{19,11},{27,3},{4,28},{... | collective-permute-start | bytes 638984 | tf_op jit(solution)/shard_map/ppermute | solution.py:475
  33.1 0.7 %collective-permute-start.8 = (bf16[400,256]{1,0:T(8,128)(2,1)S(1)}, bf16[400,256]{1,0:T(8,128)(2,1)S(1)}, u32[]{:S(2)}, u32[]{:S(2)}) collective-permute-start(bf16[400,256]{1,0:T(8,128)(2,1)S(1)} %get-tuple-element.36), channel_id=1, source_target_pairs={{0,8},{8,0},{17,25},{25,17},{2,10},{10,2},{19,27},{27,19},{4,12},{... | collective-permute-start | bytes 614408 | tf_op jit(solution)/shard_map/ppermute | solution.py:475
  33.8 1.3 %collective-permute-start.9 = (bf16[384,256]{1,0:T(8,128)(2,1)S(1)}, bf16[384,256]{1,0:T(8,128)(2,1)S(1)}, u32[]{:S(2)}, u32[]{:S(2)}) collective-permute-start(bf16[384,256]{1,0:T(8,128)(2,1)S(1)} %get-tuple-element.37), channel_id=1, source_target_pairs={{0,16},{8,24},{17,1},{25,9},{2,18},{10,26},{19,3},{27,11},{4,20},{... | collective-permute-start | bytes 589832 | tf_op jit(solution)/shard_map/ppermute | solution.py:475
  35.1 12.8 %collective-permute-done.9.refs_2_ = bf16[384,256]{1,0:T(8,128)(2,1)S(1)} collective-permute-done((bf16[384,256]{1,0:T(8,128)(2,1)S(1)}, bf16[384,256]{1,0:T(8,128)(2,1)S(1)}, u32[]{:S(2)}, u32[]{:S(2)}) %collective-permute-start.9) | collective-permute-done | bytes 196640 | tf_op jit(solution)/shard_map/ppermute | solution.py:475
  47.9 0.0 collective-permute-done.8.refs_1_
  47.9 0.0 collective-permute-done.10.refs_3_
  47.9 0.9 %place.1 = (bf16[384,256]{1,0:T(8,128)(2,1)S(1)}, f32[384,256]{1,0:T(8,128)S(1)}) custom-call(s32[2]{0:T(128)S(1)} %copy-done.1, bf16[384,256]{1,0:T(8,128)(2,1)S(1)} %get-tuple-element.35.refs_0_, bf16[400,256]{1,0:T(8,128)(2,1)S(1)} %collective-permute-done.8.refs_1_, bf16[384,256]{1,0:T(8,128)(2,1)S(1)} %collective-permute-done.9.refs_2_, ...), custom_call_target="tpu_custom_call" | custom-call | tf_op jit(solution)/shard_map/place/pallas_call | solution.py:477
  48.8 2.4 %collective-permute-start.11 = (bf16[384,256]{1,0:T(8,128)(2,1)S(1)}, bf16[384,256]{1,0:T(8,128)(2,1)S(1)}, u32[]{:S(2)}, u32[]{:S(2)}) collective-permute-start(bf16[384,256]{1,0:T(8,128)(2,1)S(1)} %get-tuple-element.40), channel_id=1, source_target_pairs={{1,0},{2,1},{3,2},{4,3},{5,4},{6,5},{7,6},{9,8},{10,9},{11,10},{12... | collective-permute-start | bytes 589832 | tf_op jit(solution)/shard_map/ppermute | solution.py:485
  51.2 4.5 %collective-permute-done.11 = bf16[384,256]{1,0:T(8,128)(2,1)S(1)} collective-permute-done((bf16[384,256]{1,0:T(8,128)(2,1)S(1)}, bf16[384,256]{1,0:T(8,128)(2,1)S(1)}, u32[]{:S(2)}, u32[]{:S(2)}) %collective-permute-start.11) | collective-permute-done | bytes 196640 | tf_op jit(solution)/shard_map/ppermute | solution.py:485
  55.8 0.8 %convert_add_fusion = f32[384,256]{1,0:T(8,128)} fusion(f32[384,256]{1,0:T(8,128)S(1)} %get-tuple-element.39, bf16[384,256]{1,0:T(8,128)(2,1)S(1)} %collective-permute-done.11), kind=kLoop, calls=%fused_computation | loop fusion | flops 196608 | bytes 983040 | tf_op jit(solution)/shard_map/add | solution.py:486
  (4 shorter events, 0.0 us)
Async XLA Ops:
  0.0 10.8 %collective-permute-start = (bf16[384,256]{1,0:T(8,128)(2,1)}, bf16[384,256]{1,0:T(8,128)(2,1)S(1)}, u32[]{:S(2)}, u32[]{:S(2)}) collective-permute-start(bf16[384,256]{1,0:T(8,128)(2,1)} %bitcast.8), channel_id=1, source_target_pairs={{0,1},{1,2},{2,3},{3,4},{4,5},{5,6},{6,7},{8,9},{9,10},{10,11},{11... | collective-permute-start | bytes 589832 | tf_op jit(solution)/shard_map/ppermute | solution.py:368
  6.0 11.1 %collective-permute-start.4 = (bf16[960,256]{1,0:T(8,128)(2,1)S(1)}, bf16[960,256]{1,0:T(8,128)(2,1)S(1)}, u32[]{:S(2)}, u32[]{:S(2)}) collective-permute-start(bf16[960,256]{1,0:T(8,128)(2,1)S(1)} %get-tuple-element.29), channel_id=1, source_target_pairs={{24,0},{16,8},{9,17},{1,25},{26,2},{18,10},{11,19},{3,27},{28,4},{... | collective-permute-start | bytes 1474568 | tf_op jit(solution)/shard_map/ppermute | solution.py:393
  12.0 15.7 %collective-permute-start.2 = (bf16[1760,256]{1,0:T(8,128)(2,1)S(1)}, bf16[1760,256]{1,0:T(8,128)(2,1)S(1)}, u32[]{:S(2)}, u32[]{:S(2)}) collective-permute-start(bf16[1760,256]{1,0:T(8,128)(2,1)S(1)} %get-tuple-element.25.refs_0_), channel_id=1, source_target_pairs={{16,0},{24,8},{1,17},{9,25},{18,2},{26,10},{3,19},{11,27},{20,4},{... | collective-permute-start | bytes 2703368 | tf_op jit(solution)/shard_map/ppermute | solution.py:412
  13.3 8.2 %collective-permute-start.3 = (bf16[400,256]{1,0:T(8,128)(2,1)S(1)}, bf16[400,256]{1,0:T(8,128)(2,1)S(1)}, u32[]{:S(2)}, u32[]{:S(2)}) collective-permute-start(bf16[400,256]{1,0:T(8,128)(2,1)S(1)} %get-tuple-element.28), channel_id=1, source_target_pairs={{24,0},{16,8},{9,17},{1,25},{26,2},{18,10},{11,19},{3,27},{28,4},{... | collective-permute-start | bytes 614408 | tf_op jit(solution)/shard_map/ppermute | solution.py:414
  14.6 12.7 %collective-permute-start.1 = (bf16[1680,256]{1,0:T(8,128)(2,1)S(1)}, bf16[1680,256]{1,0:T(8,128)(2,1)S(1)}, u32[]{:S(2)}, u32[]{:S(2)}) collective-permute-start(bf16[1680,256]{1,0:T(8,128)(2,1)S(1)} %get-tuple-element.26), channel_id=1, source_target_pairs={{8,0},{0,8},{25,17},{17,25},{10,2},{2,10},{27,19},{19,27},{12,4},{... | collective-permute-start | bytes 2580488 | tf_op jit(solution)/shard_map/ppermute | solution.py:411
  17.1 10.1 %collective-permute-start.5 = (bf16[960,256]{1,0:T(8,128)(2,1)S(1)}, bf16[960,256]{1,0:T(8,128)(2,1)S(1)}, u32[]{:S(2)}, u32[]{:S(2)}) collective-permute-start(bf16[960,256]{1,0:T(8,128)(2,1)S(1)} %collective-permute-done.4.first_ref), channel_id=1, source_target_pairs={{0,2},{8,10},{17,19},{25,27},{2,0},{10,8},{19,17},{27,25},{4,6},{1... | collective-permute-start | bytes 1474568 | tf_op jit(solution)/shard_map/ppermute | solution.py:415
  21.5 6.1 %copy-start = (bf16[2,2,128,256]{3,2,1,0:T(8,128)(2,1)S(1)}, bf16[2,2,128,256]{3,2,1,0:T(8,128)(2,1)}, u32[]{:S(2)}) copy-start(bf16[2,2,128,256]{3,2,1,0:T(8,128)(2,1)} %param.6) | copy-start | bytes 786436
  21.5 9.6 %collective-permute-start.7 = (bf16[640,256]{1,0:T(8,128)(2,1)S(1)}, bf16[640,256]{1,0:T(8,128)(2,1)S(1)}, u32[]{:S(2)}, u32[]{:S(2)}) collective-permute-start(bf16[640,256]{1,0:T(8,128)(2,1)S(1)} %hold.1.refs_3_), channel_id=1, source_target_pairs={{16,0},{24,8},{1,17},{9,25},{18,2},{26,10},{3,19},{11,27},{20,4},{... | collective-permute-start | bytes 983048 | tf_op jit(solution)/shard_map/ppermute | solution.py:426
  25.9 5.3 %collective-permute-start.6 = (bf16[640,256]{1,0:T(8,128)(2,1)S(1)}, bf16[640,256]{1,0:T(8,128)(2,1)S(1)}, u32[]{:S(2)}, u32[]{:S(2)}) collective-permute-start(bf16[640,256]{1,0:T(8,128)(2,1)S(1)} %hold.1.refs_3_), channel_id=1, source_target_pairs={{9,0},{1,8},{24,17},{16,25},{11,2},{3,10},{26,19},{18,27},{13,4},{... | collective-permute-start | bytes 983048 | tf_op jit(solution)/shard_map/ppermute | solution.py:426
  31.2 16.6 %copy-start.1 = (s32[2]{0:T(128)S(1)}, s32[2]{0:T(128)}, u32[]{:S(2)}) copy-start(s32[2]{0:T(128)} %anchors.1) | copy-start | bytes 28
  31.8 16.1 %collective-permute-start.10 = (bf16[416,256]{1,0:T(8,128)(2,1)S(1)}, bf16[416,256]{1,0:T(8,128)(2,1)S(1)}, u32[]{:S(2)}, u32[]{:S(2)}) collective-permute-start(bf16[416,256]{1,0:T(8,128)(2,1)S(1)} %get-tuple-element.38), channel_id=1, source_target_pairs={{0,24},{8,16},{17,9},{25,1},{2,26},{10,18},{19,11},{27,3},{4,28},{... | collective-permute-start | bytes 638984 | tf_op jit(solution)/shard_map/ppermute | solution.py:475
  33.1 14.7 %collective-permute-start.8 = (bf16[400,256]{1,0:T(8,128)(2,1)S(1)}, bf16[400,256]{1,0:T(8,128)(2,1)S(1)}, u32[]{:S(2)}, u32[]{:S(2)}) collective-permute-start(bf16[400,256]{1,0:T(8,128)(2,1)S(1)} %get-tuple-element.36), channel_id=1, source_target_pairs={{0,8},{8,0},{17,25},{25,17},{2,10},{10,2},{19,27},{27,19},{4,12},{... | collective-permute-start | bytes 614408 | tf_op jit(solution)/shard_map/ppermute | solution.py:475
  33.8 14.1 %collective-permute-start.9 = (bf16[384,256]{1,0:T(8,128)(2,1)S(1)}, bf16[384,256]{1,0:T(8,128)(2,1)S(1)}, u32[]{:S(2)}, u32[]{:S(2)}) collective-permute-start(bf16[384,256]{1,0:T(8,128)(2,1)S(1)} %get-tuple-element.37), channel_id=1, source_target_pairs={{0,16},{8,24},{17,1},{25,9},{2,18},{10,26},{19,3},{27,11},{4,20},{... | collective-permute-start | bytes 589832 | tf_op jit(solution)/shard_map/ppermute | solution.py:475
  48.8 7.0 %collective-permute-start.11 = (bf16[384,256]{1,0:T(8,128)(2,1)S(1)}, bf16[384,256]{1,0:T(8,128)(2,1)S(1)}, u32[]{:S(2)}, u32[]{:S(2)}) collective-permute-start(bf16[384,256]{1,0:T(8,128)(2,1)S(1)} %get-tuple-element.40), channel_id=1, source_target_pairs={{1,0},{2,1},{3,2},{4,3},{5,4},{6,5},{7,6},{9,8},{10,9},{11,10},{12... | collective-permute-start | bytes 589832 | tf_op jit(solution)/shard_map/ppermute | solution.py:485
where the time goes:
time: 57 us; the launch traced here: 56.5 us
  waiting for transfers between devices  26 us (46%)
  starting transfers between devices  24.1 us (42%)
  Pallas kernels  4.75 us (8%)
  between operations  0.82 us (1%)
  other arithmetic  0.78 us (1%)
    ppermute x3, waiting for transfers between devices, on_device(): lax.ppermute(correlations[r], BOTH, plan.from_workers(r))  12.8 us
    ppermute x2, starting transfers between devices, on_device(): lates = [lax.ppermute(late, BOTH, plan.ops_to_workers(r)) for r in (1, 2)]  5.71 us
    ppermute x1, starting transfers between devices, on_device(): lax.ppermute(tile_reflect, 'tile', [(i, i + 1) for i in range(plan.tiles...  4.58 us
    ppermute x1, waiting for transfers between devices, on_device(): lax.ppermute(left, 'tile', [(i + 1, i) for i in range(plan.tiles - 1)])  4.54 us
    ppermute x1, starting transfers between devices, on_device(): far_half = lax.ppermute(far_half, BOTH, plan.to_workers(last))  4.1 us
    ppermute x1, waiting for transfers between devices, on_device(): far_window = lax.ppermute(far_window, BOTH, plan.to_workers(last))  3.7 us
    ppermute x3, starting transfers between devices, on_device(): lax.ppermute(correlations[r], BOTH, plan.from_workers(r))  3.26 us
    ppermute x2, waiting for transfers between devices, on_device(): lates = [lax.ppermute(late, BOTH, plan.ops_to_workers(r)) for r in (1, 2)]  2.98 us
  transfers between devices with their start and end apart: 12, of which 7 were waited for; matrix products, arithmetic and copies ran while one was open for 0% of the time, Pallas kernels for 6%

commit v1 on v0

--- a/solution.py
+++ b/solution.py
@@ -58,15 +58,18 @@
         return [(b, a) for a, b in self.to_workers(r)]
 
 
-def pack_kernel(group, sizes, x_hbm, y_hbm, even, odd, late, half_out, x_ref, y_ref, sem):
+def pack_kernel(group, sizes, x_hbm, y_hbm, reflect_hbm, anchors_hbm, *refs):
     slots, rows, columns = sizes
+    even, odd, late, half_out, reflect, anchors, x_ref, y_ref, sem = refs
     loads = [
         pltpu.make_async_copy(x_hbm, x_ref, sem.at[0]),
         pltpu.make_async_copy(y_hbm, y_ref, sem.at[1]),
+        pltpu.make_async_copy(reflect_hbm, reflect, sem.at[2]),
+        pltpu.make_async_copy(anchors_hbm, anchors, sem.at[3]),
     ]
     for load in loads:
         load.start()
-    for load in loads:
+    for load in loads[:2]:
         load.wait()
     piece = rows // 2
     part = columns + piece
@@ -87,19 +90,13 @@
     plane = lax.rem(lax.axis_index("tile") // group, 2)
     half_out[:first, :] = even[pl.ds(pl.multiple_of(plane * first, first), first), :]
     half_out[first:, :] = late[pl.ds(pl.multiple_of(plane * part, part), part), :]
-
-
-def window_kernel(shots, sizes, anchors_hbm, counts, left_ref, right_hbm, *refs):
+    for load in loads[2:]:
+        load.wait()
+
+
+def window_kernel(shots, sizes, anchors, counts, left_ref, right_ref, *refs):
     slots, rows, columns = sizes
-    messages, (alone, anchors, right_ref, sem) = refs[shots : 2 * shots], refs[2 * shots :]
-    loads = [
-        pltpu.make_async_copy(anchors_hbm, anchors, sem.at[0]),
-        pltpu.make_async_copy(right_hbm, right_ref, sem.at[1]),
-    ]
-    for load in loads:
-        load.start()
-    for load in loads:
-        load.wait()
+    messages, alone = refs[shots : 2 * shots], refs[2 * shots]
     section, tile = lax.axis_index("depth"), lax.axis_index("tile")
     left, right = left_ref[...].astype(jnp.float32), right_ref[...].astype(jnp.float32)
     lanes = lax.broadcasted_iota(jnp.int32, left.shape, 1)
@@ -319,11 +316,12 @@
     pass
 
 
-def place_kernel(shots, anchors, *refs):
-    arrived, (left_out, own_out) = refs[:-2], refs[-2:]
+def place_kernel(shots, to_left, anchors, *refs):
+    arrived, out = refs[:-1], refs[-1]
     section, tile = lax.axis_index("depth"), lax.axis_index("tile")
-    places, columns = left_out.shape
-    left_sum, own_sum = None, None
+    places, columns = out.shape
+    lanes = lax.broadcasted_iota(jnp.int32, out.shape, 1)
+    placed = None
     for q in range(shots):
         offset = anchors[lax.rem(section, shots) ^ q] - (tile - 1) * columns
         total = None
@@ -331,13 +329,10 @@
             value = arrived[r][:places, :].astype(jnp.float32)
             total = value if total is None else total + value
         turned = pltpu.roll(total, lax.rem(offset, columns), 1)
-        lanes = lax.broadcasted_iota(jnp.int32, turned.shape, 1)
-        left = jnp.where(lanes >= offset, turned, 0.0)
-        own = jnp.where(lanes >= offset, 0.0, turned)
-        left_sum = left if left_sum is None else left_sum + left
-        own_sum = own if own_sum is None else own_sum + own
-    left_out[...] = left_sum.astype(left_out.dtype)
-    own_out[...] = own_sum
+        chosen = lanes >= offset if to_left else lanes < offset
+        part = jnp.where(chosen, turned, 0.0)
+        placed = part if placed is None else placed + part
+    out[...] = placed.astype(out.dtype)
 
 
 def kept(array):
@@ -371,41 +366,38 @@
     early_rows = 2 * (half_rows - part) + win_rows
     even = pltpu.VMEM((early_rows + 5 * TAIL, columns), bf16)
     odd = pltpu.VMEM((early_rows, columns), bf16)
-    even_early, odd_early, late, far_half = pl.pallas_call(
+    even_early, odd_early, late, far_half, own_reflect, near_anchors = pl.pallas_call(
         functools.partial(pack_kernel, group, sizes),
         out_shape=[
             even,
             odd,
             jax.ShapeDtypeStruct((2 * part, columns), bf16),
             jax.ShapeDtypeStruct((half_rows, columns), bf16),
+            pltpu.VMEM(tile_reflect.shape, bf16),
+            jax.ShapeDtypeStruct(anchors.shape, jnp.int32),
         ],
-        in_specs=[hbm, hbm],
-        out_specs=[vmem] * 4,
+        in_specs=[hbm] * 4,
+        out_specs=[vmem] * 5 + [smem],
         scratch_shapes=[
             pltpu.VMEM(lateral_x.shape[1:], bf16),
             pltpu.VMEM(lateral_y.shape[1:], bf16),
-            pltpu.SemaphoreType.DMA((2,)),
+            pltpu.SemaphoreType.DMA((4,)),
         ],
         compiler_params=params(12),
         name="pack",
-    )(kept(lateral_x[0]), kept(lateral_y[0]))
+    )(kept(lateral_x[0]), kept(lateral_y[0]), kept(tile_reflect), kept(anchors))
     last = sections - 1
     far_half = lax.ppermute(far_half, BOTH, plan.to_workers(last))
     even_early, odd_early, far_window = pl.pallas_call(
         functools.partial(window_kernel, shots, sizes),
         out_shape=[even, odd, jax.ShapeDtypeStruct((win_rows, columns), bf16)],
-        in_specs=[hbm, smem, vmem, hbm, vmem, vmem],
+        in_specs=[smem, smem] + [vmem] * 4,
         out_specs=[vmem] * 3,
-        scratch_shapes=[
-            pltpu.SMEM((shots,), jnp.int32),
-            pltpu.VMEM((slots * rows, columns), bf16),
-            pltpu.SemaphoreType.DMA((2,)),
-        ],
         input_output_aliases={4: 0, 5: 1},
         compiler_params=params(12),
         cost_estimate=pl.CostEstimate(flops=3 * 10**9, bytes_accessed=4 * MIB, transcendentals=0),
         name="windows",
-    )(kept(anchors), counts, halo, kept(tile_reflect), held(even_early), held(odd_early))
+    )(near_anchors, counts, halo, held(own_reflect), held(even_early), held(odd_early))
     messages = [
         even_early,
         lax.ppermute(odd_early, BOTH, plan.to_workers(1)),
@@ -470,18 +462,20 @@
         *[held(buffer) for buffer in filled],
     )
 
-    corr_shape = jax.ShapeDtypeStruct((slots * rows, columns), bf16)
     arrived = [correlations[0]] + [
         lax.ppermute(correlations[r], BOTH, plan.from_workers(r)) for r in range(1, sections)
     ]
-    left, own = pl.pallas_call(
-        functools.partial(place_kernel, shots),
-        out_shape=[corr_shape, jax.ShapeDtypeStruct((slots * rows, columns), jnp.float32)],
-        in_specs=[smem] + [vmem] * sections,
-        out_specs=[vmem, vmem],
-        compiler_params=params(8),
-        name="place",
-    )(anchors, *arrived)
+    left, own = [
+        pl.pallas_call(
+            functools.partial(place_kernel, shots, to_left),
+            out_shape=jax.ShapeDtypeStruct((slots * rows, columns), kind),
+            in_specs=[smem] + [vmem] * sections,
+            out_specs=vmem,
+            compiler_params=params(8),
+            name=name,
+        )(near_anchors, *arrived)
+        for to_left, kind, name in ((True, bf16, "left"), (False, jnp.float32, "own"))
+    ]
     from_right = lax.ppermute(left, "tile", [(i + 1, i) for i in range(plan.tiles - 1)])
     image = own + from_right.astype(jnp.float32)
     return image.reshape(1, slots, rows, columns)

time: 57 us -> 57 us (level); the launches traced: 56.5 us -> 57.4 us
  Pallas kernels: 4.75 us -> 5.8 us
    pallas_call x1 -> x2, Pallas kernels: 0.89 us -> 1.69 us  [on_device(): pl.pallas_call(functools.partial(place_kernel, shots, to_left), out_shape...]
    ppermute x1, waiting for transfers between devices: 1.77 us -> 2.57 us  [on_device(): far_half = lax.ppermute(far_half, BOTH, plan.to_workers(last))]
    pallas_call x1, Pallas kernels: 1.4 us -> 2.02 us  [on_device(): pl.pallas_call(functools.partial(pack_kernel, group, sizes), out_shape=[e...]
  transfers between devices with their start and end apart: 12 -> 12, of which waited for: 7 -> 6; matrix products, arithmetic and copies ran while one was open for 0% -> 0% of each run, Pallas kernels for 6% -> 8%
where the time goes in v1:
time: 57 us; the launch traced here: 57.4 us
  waiting for transfers between devices  26.2 us (46%)
  starting transfers between devices  23.7 us (42%)
  Pallas kernels  5.8 us (10%)
  between operations  0.84 us (1%)
  other arithmetic  0.79 us (1%)
    ppermute x3, waiting for transfers between devices, on_device(): lax.ppermute(correlations[r], BOTH, plan.from_workers(r))  12.6 us
    ppermute x2, starting transfers between devices, on_device(): lates = [lax.ppermute(late, BOTH, plan.ops_to_workers(r)) for r in (1, 2)]  5.71 us
    ppermute x1, starting transfers between devices, on_device(): lax.ppermute(tile_reflect, 'tile', [(i, i + 1) for i in range(plan.tiles...  4.58 us
    ppermute x1, waiting for transfers between devices, on_device(): lax.ppermute(left, 'tile', [(i + 1, i) for i in range(plan.tiles - 1)])  4.16 us
    ppermute x1, starting transfers between devices, on_device(): far_half = lax.ppermute(far_half, BOTH, plan.to_workers(last))  4.1 us
    ppermute x1, waiting for transfers between devices, on_device(): far_window = lax.ppermute(far_window, BOTH, plan.to_workers(last))  3.7 us
    ppermute x3, starting transfers between devices, on_device(): lax.ppermute(correlations[r], BOTH, plan.from_workers(r))  3.26 us
    ppermute x2, waiting for transfers between devices, on_device(): lates = [lax.ppermute(late, BOTH, plan.ops_to_workers(r)) for r in (1, 2)]  3.21 us
  transfers between devices with their start and end apart: 12, of which 6 were waited for; matrix products, arithmetic and copies ran while one was open for 0% of the time, Pallas kernels for 8%

profile of v1, /device:TPU:1, one launch (start us, length us, event | category | flops | bytes accessed | tf_op | source)
XLA Modules:
  0.0 57.4 jit_solution(16331128398599251690)
XLA Ops:
  0.0 4.6 %collective-permute-start = (bf16[384,256]{1,0:T(8,128)(2,1)}, bf16[384,256]{1,0:T(8,128)(2,1)S(1)}, u32[]{:S(2)}, u32[]{:S(2)}) collective-permute-start(bf16[384,256]{1,0:T(8,128)(2,1)} %bitcast.8), channel_id=1, source_target_pairs={{0,1},{1,2},{2,3},{3,4},{4,5},{5,6},{6,7},{8,9},{9,10},{10,11},{11... | collective-permute-start | bytes 589832 | tf_op jit(solution)/shard_map/ppermute | solution.py:363
  4.6 2.0 %pack.1 = (bf16[1760,256]{1,0:T(8,128)(2,1)S(1)}, bf16[1680,256]{1,0:T(8,128)(2,1)S(1)}, bf16[640,256]{1,0:T(8,128)(2,1)S(1)}, bf16[960,256]{1,0:T(8,128)(2,1)S(...) custom-call(bf16[3,2,128,128]{3,2,1,0:T(8,128)(2,1)} %bitcast.7, bf16[3,2,256,256]{3,2,1,0:T(8,128)(2,1)} %bitcast.6, ...), custom_call_target="tpu_custom_call" | custom-call | tf_op jit(solution)/shard_map/pack/pallas_call | solution.py:369
  6.6 4.1 %collective-permute-start.4 = (bf16[960,256]{1,0:T(8,128)(2,1)S(1)}, bf16[960,256]{1,0:T(8,128)(2,1)S(1)}, u32[]{:S(2)}, u32[]{:S(2)}) collective-permute-start(bf16[960,256]{1,0:T(8,128)(2,1)S(1)} %get-tuple-element.31), channel_id=1, source_target_pairs={{24,0},{16,8},{9,17},{1,25},{26,2},{18,10},{11,19},{3,27},{28,4},{... | collective-permute-start | bytes 1474568 | tf_op jit(solution)/shard_map/ppermute | solution.py:390
  11.4 0.0 collective-permute-done.left_ref
  11.4 0.8 %windows.1 = (bf16[1760,256]{1,0:T(8,128)(2,1)S(1)}, bf16[1680,256]{1,0:T(8,128)(2,1)S(1)}, bf16[400,256]{1,0:T(8,128)(2,1)S(1)}) custom-call(s32[2]{0:T(128)S(1)} %get-tuple-element.23.anchors, s32[1]{0:T(128)S(6)} %copy.21.counts, bf16[384,256]{1,0:T(8,128)(2,1)S(1)} %collective-permute-done.left_ref, ...), custom_call_target="tpu_custom_call", output_to_operand_aliasing={{0}: (4, {}), {1}: (5, {})} | custom-call | flops 3000000000 | bytes 4194304 | tf_op jit(solution)/shard_map/windows/pallas_call | solution.py:391
  12.2 1.3 %collective-permute-start.2 = (bf16[1760,256]{1,0:T(8,128)(2,1)S(1)}, bf16[1760,256]{1,0:T(8,128)(2,1)S(1)}, u32[]{:S(2)}, u32[]{:S(2)}) collective-permute-start(bf16[1760,256]{1,0:T(8,128)(2,1)S(1)} %get-tuple-element.27.refs_0_), channel_id=1, source_target_pairs={{16,0},{24,8},{1,17},{9,25},{18,2},{26,10},{3,19},{11,27},{20,4},{... | collective-permute-start | bytes 2703368 | tf_op jit(solution)/shard_map/ppermute | solution.py:404
  13.6 1.3 %collective-permute-start.3 = (bf16[400,256]{1,0:T(8,128)(2,1)S(1)}, bf16[400,256]{1,0:T(8,128)(2,1)S(1)}, u32[]{:S(2)}, u32[]{:S(2)}) collective-permute-start(bf16[400,256]{1,0:T(8,128)(2,1)S(1)} %get-tuple-element.30), channel_id=1, source_target_pairs={{24,0},{16,8},{9,17},{1,25},{26,2},{18,10},{11,19},{3,27},{28,4},{... | collective-permute-start | bytes 614408 | tf_op jit(solution)/shard_map/ppermute | solution.py:406
  14.9 0.7 %collective-permute-start.1 = (bf16[1680,256]{1,0:T(8,128)(2,1)S(1)}, bf16[1680,256]{1,0:T(8,128)(2,1)S(1)}, u32[]{:S(2)}, u32[]{:S(2)}) collective-permute-start(bf16[1680,256]{1,0:T(8,128)(2,1)S(1)} %get-tuple-element.28), channel_id=1, source_target_pairs={{8,0},{0,8},{25,17},{17,25},{10,2},{2,10},{27,19},{19,27},{12,4},{... | collective-permute-start | bytes 2580488 | tf_op jit(solution)/shard_map/ppermute | solution.py:403
  15.6 2.6 %collective-permute-done.4.first_ref = bf16[960,256]{1,0:T(8,128)(2,1)S(1)} collective-permute-done((bf16[960,256]{1,0:T(8,128)(2,1)S(1)}, bf16[960,256]{1,0:T(8,128)(2,1)S(1)}, u32[]{:S(2)}, u32[]{:S(2)}) %collective-permute-start.4) | collective-permute-done | bytes 491552 | tf_op jit(solution)/shard_map/ppermute | solution.py:390
  18.2 0.7 %collective-permute-start.5 = (bf16[960,256]{1,0:T(8,128)(2,1)S(1)}, bf16[960,256]{1,0:T(8,128)(2,1)S(1)}, u32[]{:S(2)}, u32[]{:S(2)}) collective-permute-start(bf16[960,256]{1,0:T(8,128)(2,1)S(1)} %collective-permute-done.4.first_ref), channel_id=1, source_target_pairs={{0,2},{8,10},{17,19},{25,27},{2,0},{10,8},{19,17},{27,25},{4,6},{1... | collective-permute-start | bytes 1474568 | tf_op jit(solution)/shard_map/ppermute | solution.py:407
  18.9 3.7 %collective-permute-done.3.after_ref.refs_5_.refs_7_ = bf16[400,256]{1,0:T(8,128)(2,1)S(1)} collective-permute-done((bf16[400,256]{1,0:T(8,128)(2,1)S(1)}, bf16[400,256]{1,0:T(8,128)(2,1)S(1)}, u32[]{:S(2)}, u32[]{:S(2)}) %collective-permute-start.3) | collective-permute-done | bytes 204832 | tf_op jit(solution)/shard_map/ppermute | solution.py:406
  22.6 4.4 %collective-permute-start.7 = (bf16[640,256]{1,0:T(8,128)(2,1)S(1)}, bf16[640,256]{1,0:T(8,128)(2,1)S(1)}, u32[]{:S(2)}, u32[]{:S(2)}) collective-permute-start(bf16[640,256]{1,0:T(8,128)(2,1)S(1)} %hold.1.refs_3_), channel_id=1, source_target_pairs={{16,0},{24,8},{1,17},{9,25},{18,2},{26,10},{3,19},{11,27},{20,4},{... | collective-permute-start | bytes 983048 | tf_op jit(solution)/shard_map/ppermute | solution.py:418
  27.0 1.3 %collective-permute-start.6 = (bf16[640,256]{1,0:T(8,128)(2,1)S(1)}, bf16[640,256]{1,0:T(8,128)(2,1)S(1)}, u32[]{:S(2)}, u32[]{:S(2)}) collective-permute-start(bf16[640,256]{1,0:T(8,128)(2,1)S(1)} %hold.1.refs_3_), channel_id=1, source_target_pairs={{9,0},{1,8},{24,17},{16,25},{11,2},{3,10},{26,19},{18,27},{13,4},{... | collective-permute-start | bytes 983048 | tf_op jit(solution)/shard_map/ppermute | solution.py:418
  28.3 0.0 collective-permute-done.5.second_ref
  28.3 0.1 join.1.refs_4_.refs_6_
  28.4 0.0 collective-permute-done.1.refs_1_
  28.4 0.0 collective-permute-done.2.refs_2_
  28.4 0.6 %down.1 = (bf16[12,512,256]{2,1,0:T(8,128)(2,1)S(1)}, bf16[12,256,256]{2,1,0:T(8,128)(2,1)S(1)}, bf16[12,128,256]{2,1,0:T(8,128)(2,1)S(1)}, bf16[13,256,256]{2,1,0:T(8,128)(2,1)S(1)}, s32[7]{0:T(128)S(1)}) custom-call(bf16[2,256,256]{2,1,0:T(8,128)(2,1)S(1)} %bitcast.5, bf16[1760,256]{1,0:T(8,128)(2,1)S(1)} %get-tuple-element.27.refs_0_, ...), custom_call_target="tpu_custom_call" | custom-call | tf_op jit(solution)/shard_map/down/pallas_call | solution.py:438
  29.1 2.7 %collective-permute-done.7.refs_5_ = bf16[640,256]{1,0:T(8,128)(2,1)S(1)} collective-permute-done((bf16[640,256]{1,0:T(8,128)(2,1)S(1)}, bf16[640,256]{1,0:T(8,128)(2,1)S(1)}, u32[]{:S(2)}, u32[]{:S(2)}) %collective-permute-start.7) | collective-permute-done | bytes 327712 | tf_op jit(solution)/shard_map/ppermute | solution.py:418
  31.8 0.5 collective-permute-done.6.refs_4_
  32.3 0.6 up.1
  32.8 1.3 %collective-permute-start.10 = (bf16[416,256]{1,0:T(8,128)(2,1)S(1)}, bf16[416,256]{1,0:T(8,128)(2,1)S(1)}, u32[]{:S(2)}, u32[]{:S(2)}) collective-permute-start(bf16[416,256]{1,0:T(8,128)(2,1)S(1)} %get-tuple-element.40), channel_id=1, source_target_pairs={{0,24},{8,16},{17,9},{25,1},{2,26},{10,18},{19,11},{27,3},{4,28},{... | collective-permute-start | bytes 638984 | tf_op jit(solution)/shard_map/ppermute | solution.py:466
  34.1 0.7 %collective-permute-start.8 = (bf16[400,256]{1,0:T(8,128)(2,1)S(1)}, bf16[400,256]{1,0:T(8,128)(2,1)S(1)}, u32[]{:S(2)}, u32[]{:S(2)}) collective-permute-start(bf16[400,256]{1,0:T(8,128)(2,1)S(1)} %get-tuple-element.38), channel_id=1, source_target_pairs={{0,8},{8,0},{17,25},{25,17},{2,10},{10,2},{19,27},{27,19},{4,12},{... | collective-permute-start | bytes 614408 | tf_op jit(solution)/shard_map/ppermute | solution.py:466
  34.8 1.3 %collective-permute-start.9 = (bf16[384,256]{1,0:T(8,128)(2,1)S(1)}, bf16[384,256]{1,0:T(8,128)(2,1)S(1)}, u32[]{:S(2)}, u32[]{:S(2)}) collective-permute-start(bf16[384,256]{1,0:T(8,128)(2,1)S(1)} %get-tuple-element.39), channel_id=1, source_target_pairs={{0,16},{8,24},{17,1},{25,9},{2,18},{10,26},{19,3},{27,11},{4,20},{... | collective-permute-start | bytes 589832 | tf_op jit(solution)/shard_map/ppermute | solution.py:466
  36.1 12.6 %collective-permute-done.9.refs_2_ = bf16[384,256]{1,0:T(8,128)(2,1)S(1)} collective-permute-done((bf16[384,256]{1,0:T(8,128)(2,1)S(1)}, bf16[384,256]{1,0:T(8,128)(2,1)S(1)}, u32[]{:S(2)}, u32[]{:S(2)}) %collective-permute-start.9) | collective-permute-done | bytes 196640 | tf_op jit(solution)/shard_map/ppermute | solution.py:466
  48.7 0.0 collective-permute-done.8.refs_1_
  48.7 0.0 collective-permute-done.10.refs_3_
  48.7 0.8 %left.1 = bf16[384,256]{1,0:T(8,128)(2,1)S(1)} custom-call(s32[2]{0:T(128)S(1)} %get-tuple-element.23.anchors, bf16[384,256]{1,0:T(8,128)(2,1)S(1)} %get-tuple-element.37.refs_0_, bf16[400,256]{1,0:T(8,128)(2,1)S(1)} %collective-permute-done.8.refs_1_, bf16[384,256]{1,0:T(8,128)(2,1)S(1)} %collective-permute-done.9.refs_2_, ...), custom_call_target="tpu_custom_call" | custom-call | tf_op jit(solution)/shard_map/left/pallas_call | solution.py:469
  49.6 2.0 %collective-permute-start.11 = (bf16[384,256]{1,0:T(8,128)(2,1)S(1)}, bf16[384,256]{1,0:T(8,128)(2,1)S(1)}, u32[]{:S(2)}, u32[]{:S(2)}) collective-permute-start(bf16[384,256]{1,0:T(8,128)(2,1)S(1)} %left.1), channel_id=1, source_target_pairs={{1,0},{2,1},{3,2},{4,3},{5,4},{6,5},{7,6},{9,8},{10,9},{11,10},{12... | collective-permute-start | bytes 589832 | tf_op jit(solution)/shard_map/ppermute | solution.py:479
  51.6 0.8 %own.1 = f32[384,256]{1,0:T(8,128)S(1)} custom-call(s32[2]{0:T(128)S(1)} %get-tuple-element.23.anchors, bf16[384,256]{1,0:T(8,128)(2,1)S(1)} %get-tuple-element.37.refs_0_, bf16[400,256]{1,0:T(8,128)(2,1)S(1)} %collective-permute-done.8.refs_1_, bf16[384,256]{1,0:T(8,128)(2,1)S(1)} %collective-permute-done.9.refs_2_, ...), custom_call_target="tpu_custom_call" | custom-call | tf_op jit(solution)/shard_map/own/pallas_call | solution.py:469
  52.4 4.2 %collective-permute-done.11 = bf16[384,256]{1,0:T(8,128)(2,1)S(1)} collective-permute-done((bf16[384,256]{1,0:T(8,128)(2,1)S(1)}, bf16[384,256]{1,0:T(8,128)(2,1)S(1)}, u32[]{:S(2)}, u32[]{:S(2)}) %collective-permute-start.11) | collective-permute-done | bytes 196640 | tf_op jit(solution)/shard_map/ppermute | solution.py:479
  56.6 0.8 %convert_add_fusion = f32[384,256]{1,0:T(8,128)} fusion(f32[384,256]{1,0:T(8,128)S(1)} %own.1, bf16[384,256]{1,0:T(8,128)(2,1)S(1)} %collective-permute-done.11), kind=kLoop, calls=%fused_computation | loop fusion | flops 196608 | bytes 983040 | tf_op jit(solution)/shard_map/add | solution.py:480
  (3 shorter events, 0.0 us)
Async XLA Ops:
  0.0 11.4 %collective-permute-start = (bf16[384,256]{1,0:T(8,128)(2,1)}, bf16[384,256]{1,0:T(8,128)(2,1)S(1)}, u32[]{:S(2)}, u32[]{:S(2)}) collective-permute-start(bf16[384,256]{1,0:T(8,128)(2,1)} %bitcast.8), channel_id=1, source_target_pairs={{0,1},{1,2},{2,3},{3,4},{4,5},{5,6},{6,7},{8,9},{9,10},{10,11},{11... | collective-permute-start | bytes 589832 | tf_op jit(solution)/shard_map/ppermute | solution.py:363
  6.6 11.5 %collective-permute-start.4 = (bf16[960,256]{1,0:T(8,128)(2,1)S(1)}, bf16[960,256]{1,0:T(8,128)(2,1)S(1)}, u32[]{:S(2)}, u32[]{:S(2)}) collective-permute-start(bf16[960,256]{1,0:T(8,128)(2,1)S(1)} %get-tuple-element.31), channel_id=1, source_target_pairs={{24,0},{16,8},{9,17},{1,25},{26,2},{18,10},{11,19},{3,27},{28,4},{... | collective-permute-start | bytes 1474568 | tf_op jit(solution)/shard_map/ppermute | solution.py:390
  12.2 16.2 %collective-permute-start.2 = (bf16[1760,256]{1,0:T(8,128)(2,1)S(1)}, bf16[1760,256]{1,0:T(8,128)(2,1)S(1)}, u32[]{:S(2)}, u32[]{:S(2)}) collective-permute-start(bf16[1760,256]{1,0:T(8,128)(2,1)S(1)} %get-tuple-element.27.refs_0_), channel_id=1, source_target_pairs={{16,0},{24,8},{1,17},{9,25},{18,2},{26,10},{3,19},{11,27},{20,4},{... | collective-permute-start | bytes 2703368 | tf_op jit(solution)/shard_map/ppermute | solution.py:404
  13.6 9.0 %collective-permute-start.3 = (bf16[400,256]{1,0:T(8,128)(2,1)S(1)}, bf16[400,256]{1,0:T(8,128)(2,1)S(1)}, u32[]{:S(2)}, u32[]{:S(2)}) collective-permute-start(bf16[400,256]{1,0:T(8,128)(2,1)S(1)} %get-tuple-element.30), channel_id=1, source_target_pairs={{24,0},{16,8},{9,17},{1,25},{26,2},{18,10},{11,19},{3,27},{28,4},{... | collective-permute-start | bytes 614408 | tf_op jit(solution)/shard_map/ppermute | solution.py:406
  14.9 13.5 %collective-permute-start.1 = (bf16[1680,256]{1,0:T(8,128)(2,1)S(1)}, bf16[1680,256]{1,0:T(8,128)(2,1)S(1)}, u32[]{:S(2)}, u32[]{:S(2)}) collective-permute-start(bf16[1680,256]{1,0:T(8,128)(2,1)S(1)} %get-tuple-element.28), channel_id=1, source_target_pairs={{8,0},{0,8},{25,17},{17,25},{10,2},{2,10},{27,19},{19,27},{12,4},{... | collective-permute-start | bytes 2580488 | tf_op jit(solution)/shard_map/ppermute | solution.py:403
  18.2 10.1 %collective-permute-start.5 = (bf16[960,256]{1,0:T(8,128)(2,1)S(1)}, bf16[960,256]{1,0:T(8,128)(2,1)S(1)}, u32[]{:S(2)}, u32[]{:S(2)}) collective-permute-start(bf16[960,256]{1,0:T(8,128)(2,1)S(1)} %collective-permute-done.4.first_ref), channel_id=1, source_target_pairs={{0,2},{8,10},{17,19},{25,27},{2,0},{10,8},{19,17},{27,25},{4,6},{1... | collective-permute-start | bytes 1474568 | tf_op jit(solution)/shard_map/ppermute | solution.py:407
  22.6 5.9 %copy-start = (bf16[2,2,128,256]{3,2,1,0:T(8,128)(2,1)S(1)}, bf16[2,2,128,256]{3,2,1,0:T(8,128)(2,1)}, u32[]{:S(2)}) copy-start(bf16[2,2,128,256]{3,2,1,0:T(8,128)(2,1)} %param.6) | copy-start | bytes 786436
  22.6 9.2 %collective-permute-start.7 = (bf16[640,256]{1,0:T(8,128)(2,1)S(1)}, bf16[640,256]{1,0:T(8,128)(2,1)S(1)}, u32[]{:S(2)}, u32[]{:S(2)}) collective-permute-start(bf16[640,256]{1,0:T(8,128)(2,1)S(1)} %hold.1.refs_3_), channel_id=1, source_target_pairs={{16,0},{24,8},{1,17},{9,25},{18,2},{26,10},{3,19},{11,27},{20,4},{... | collective-permute-start | bytes 983048 | tf_op jit(solution)/shard_map/ppermute | solution.py:418
  27.0 5.3 %collective-permute-start.6 = (bf16[640,256]{1,0:T(8,128)(2,1)S(1)}, bf16[640,256]{1,0:T(8,128)(2,1)S(1)}, u32[]{:S(2)}, u32[]{:S(2)}) collective-permute-start(bf16[640,256]{1,0:T(8,128)(2,1)S(1)} %hold.1.refs_3_), channel_id=1, source_target_pairs={{9,0},{1,8},{24,17},{16,25},{11,2},{3,10},{26,19},{18,27},{13,4},{... | collective-permute-start | bytes 983048 | tf_op jit(solution)/shard_map/ppermute | solution.py:418
  32.8 15.9 %collective-permute-start.10 = (bf16[416,256]{1,0:T(8,128)(2,1)S(1)}, bf16[416,256]{1,0:T(8,128)(2,1)S(1)}, u32[]{:S(2)}, u32[]{:S(2)}) collective-permute-start(bf16[416,256]{1,0:T(8,128)(2,1)S(1)} %get-tuple-element.40), channel_id=1, source_target_pairs={{0,24},{8,16},{17,9},{25,1},{2,26},{10,18},{19,11},{27,3},{4,28},{... | collective-permute-start | bytes 638984 | tf_op jit(solution)/shard_map/ppermute | solution.py:466
  34.1 14.6 %collective-permute-start.8 = (bf16[400,256]{1,0:T(8,128)(2,1)S(1)}, bf16[400,256]{1,0:T(8,128)(2,1)S(1)}, u32[]{:S(2)}, u32[]{:S(2)}) collective-permute-start(bf16[400,256]{1,0:T(8,128)(2,1)S(1)} %get-tuple-element.38), channel_id=1, source_target_pairs={{0,8},{8,0},{17,25},{25,17},{2,10},{10,2},{19,27},{27,19},{4,12},{... | collective-permute-start | bytes 614408 | tf_op jit(solution)/shard_map/ppermute | solution.py:466
  34.8 13.9 %collective-permute-start.9 = (bf16[384,256]{1,0:T(8,128)(2,1)S(1)}, bf16[384,256]{1,0:T(8,128)(2,1)S(1)}, u32[]{:S(2)}, u32[]{:S(2)}) collective-permute-start(bf16[384,256]{1,0:T(8,128)(2,1)S(1)} %get-tuple-element.39), channel_id=1, source_target_pairs={{0,16},{8,24},{17,1},{25,9},{2,18},{10,26},{19,3},{27,11},{4,20},{... | collective-permute-start | bytes 589832 | tf_op jit(solution)/shard_map/ppermute | solution.py:466
  49.6 7.0 %collective-permute-start.11 = (bf16[384,256]{1,0:T(8,128)(2,1)S(1)}, bf16[384,256]{1,0:T(8,128)(2,1)S(1)}, u32[]{:S(2)}, u32[]{:S(2)}) collective-permute-start(bf16[384,256]{1,0:T(8,128)(2,1)S(1)} %left.1), channel_id=1, source_target_pairs={{1,0},{2,1},{3,2},{4,3},{5,4},{6,5},{7,6},{9,8},{10,9},{11,10},{12... | collective-permute-start | bytes 589832 | tf_op jit(solution)/shard_map/ppermute | solution.py:479
